TPU v7x, 32 devices: a whole 2x2x4 slice. The times are simulated.
32 devices in a mesh: band: 4 (over x, core), dom: 8 (over z, y).
Axes of the slice: x: 2, y: 2, z: 4, core: 2. Of those that a mesh axis runs over, the one named last changes fastest.
Arguments:
- occupied: float32 [256, 12288], P('band', 'dom'), may hold values from -6 to 6
- start_guess: float32 [1, 256, 12288], P(None, 'band', 'dom'), may hold values from -0.6 to 0.6
- potential: float32 [12288], P('dom'), may hold values from 0.5 to 8
- perturbation: float32 [1, 12288], P(None, 'dom'), may hold values from -6 to 6
- band_energy: float32 [256], P('band'), may hold values from -4 to -0.5
- beta_radial: float32 [512], replicated, may hold values from -0.25 to 0.25
- beta_slope: float32 [512], replicated, may hold values from -0.25 to 0.25
- atom_owner: int32 [32], replicated, may hold values from 0 to 7, as said below
- atom_site: int32 [3, 32], replicated, may hold values from 0 to 15, as said below
- sphere_offset: int32 [3, 512], replicated, may hold values from -5 to 5
- displaced: int32 [1], replicated, may hold values from 0 to 31
Outputs:
- solution: float32 [1, 256, 12288], P(None, 'band', 'dom')
- residual: float32 [1, 256, 12288], P(None, 'band', 'dom')
Inputs may be any that keep to these rules, and one draw needn't show every extreme that they name: `atom_owner`: each slab owns at most 8 atoms and some slab owns exactly 8. `atom_site`: row 0 lies below 6, row 1 below 16, row 2 below 16. Atom 0 sits on plane 5 of its slab, row 15 and column 15; atom 1 on plane 0, row 0 and column 0.
All inputs are finite; a program needn't handle non-finite values.
Results may differ from a plain program's by a relative error of at most 0.0003.
Values sent between devices are 32-bit elements; how exact they have to be, the bound alone decides.
A program may use at most 128 MiB of HBM per device.

v0:
```python
import functools
import numpy as np
import jax
import jax.numpy as jnp
from jax import lax
from jax.experimental import pallas as pl
from jax.experimental.pallas import tpu as pltpu
from jax.sharding import PartitionSpec as P

NY = 16
NX = 16
PLANE = NY * NX
HALO = 6
CHUNKS = 8
SUM_AT = 3
RAD = 5

COEF = (
    -5369.0 / 1800.0,
    12.0 / 7.0,
    -15.0 / 56.0,
    10.0 / 189.0,
    -1.0 / 112.0,
    2.0 / 825.0,
    -1.0 / 1386.0,
)
KINETIC = 2.0
SHIFT = 20.0
STRENGTH = 10.0
HIGH = lax.Precision.HIGHEST


def plane_matrix():
    full = np.zeros((PLANE, PLANE), np.float64)
    for y in range(NY):
        for x in range(NX):
            at = y * NX + x
            full[at, at] += 3.0 * COEF[0]
            for d in range(1, 7):
                for s in (d, -d):
                    full[((y + s) % NY) * NX + x, at] += COEF[d]
                    full[y * NX + (x + s) % NX, at] += COEF[d]
    return (-KINETIC * full).astype(np.float32)


def fields_kernel(slabs, depth, radial, slope, offset, owner, site, displaced, out, padded):
    atoms = owner.shape[0]
    planes = slabs * depth
    points = offset.shape[1]
    slab = lax.axis_index("dom")
    rows = lax.broadcasted_iota(jnp.int32, (16, points), 0)
    along_z = rows == offset[0:1, :] + RAD
    in_plane = (offset[1:2, :] & (NY - 1)) * NX + (offset[2:3, :] & (NX - 1))
    hot = jnp.where(
        lax.broadcasted_iota(jnp.int32, (PLANE, points), 0) == in_plane, 1.0, 0.0
    ).astype(jnp.float32)
    left = jnp.concatenate(
        [jnp.where(along_z, radial[...], 0.0), jnp.where(along_z, slope[...], 0.0)], axis=0
    )
    template = lax.dot_general(
        left, hot, (((1,), (1,)), ((), ())), precision=HIGH, preferred_element_type=jnp.float32
    )
    padded[...] = jnp.zeros_like(padded)
    for which in range(2):
        part = template[16 * which : 16 * which + 16]
        padded[which, 0:16, :] = part
        padded[which, planes : planes + 16, :] = part
    column = lax.broadcasted_iota(jnp.int32, (8, PLANE), 1) & (NX - 1)

    def shifted(which, a):
        z = lax.rem(slab * depth + RAD + 2 * planes - owner[a] * depth - site[0, a], planes)
        x = site[2, a]
        turn = site[1, a] * NX + x
        start = pl.multiple_of(lax.div(z, 8) * 8, 8)
        block = pltpu.roll(padded[which, pl.ds(start, 16), :], lax.rem(16 - lax.rem(z, 8), 16), 0)[0:8]
        first = pltpu.roll(block, turn, 1)
        second = pltpu.roll(block, lax.rem(turn + PLANE - NX, PLANE), 1)
        return jnp.where(column >= x, first, second)

    out[atoms:, :] = jnp.zeros((out.shape[0] - atoms, out.shape[1]), jnp.float32)
    for row in range(atoms + 2):
        field = shifted(0, row) if row < atoms else shifted(row - atoms, displaced[0])
        for z in range(depth):
            out[row : row + 1, z * PLANE : (z + 1) * PLANE] = field[z : z + 1]


def atom_fields(slabs, cells, beta_radial, beta_slope, offset, owner, site, displaced):
    atoms = owner.shape[0]
    depth = cells // PLANE
    vmem = pl.BlockSpec(memory_space=pltpu.VMEM)
    smem = pl.BlockSpec(memory_space=pltpu.SMEM)
    return pl.pallas_call(
        functools.partial(fields_kernel, slabs, depth),
        out_shape=jax.ShapeDtypeStruct((max(128, atoms + 16), cells), jnp.float32),
        in_specs=[vmem, vmem, vmem, smem, smem, smem],
        out_specs=vmem,
        scratch_shapes=[pltpu.VMEM((2, slabs * depth + 16, PLANE), jnp.float32)],
        compiler_params=pltpu.CompilerParams(vmem_limit_bytes=16 * 1024 * 1024),
    )(beta_radial[None, :], beta_slope[None, :], offset, owner, site, displaced)


def times(a, b, dims):
    return lax.dot_general(a, b, (dims, ((), ())), precision=HIGH, preferred_element_type=jnp.float32)


def plain(occupied, start, potential, perturbation, energy, beta, pair, in_plane):
    slabs = lax.axis_size("dom")
    bands, cells = start.shape
    depth = cells // PLANE
    total = cells * slabs
    whole = lax.all_gather(occupied, "band", axis=0, tiled=True)
    every = whole.shape[0]
    up = [(i, (i + 1) % slabs) for i in range(slabs)]
    down = [(j, i) for i, j in up]

    def local_part(field):
        before = lax.ppermute(field, "dom", up)
        after = lax.ppermute(field, "dom", down)
        grid = jnp.concatenate([before, field, after], axis=1)
        image = times(field.reshape(bands * depth, PLANE), in_plane, ((1,), (0,))).reshape(bands, cells)
        for d in range(1, 7):
            low = (depth - d) * PLANE
            high = (depth + d) * PLANE
            image += (-KINETIC * COEF[d]) * (grid[:, low : low + cells] + grid[:, high : high + cells])
        return image + (potential - energy) * field

    def correlate(field):
        return jnp.concatenate(
            [times(field, whole, ((1,), (1,))), times(field, beta, ((1,), (1,)))], axis=1
        )

    def operator(field, total_correlation):
        return (
            local_part(field)
            + (SHIFT / total) * times(total_correlation[:, :every], whole, ((1,), (0,)))
            + STRENGTH * times(total_correlation[:, every:], beta, ((1,), (0,)))
        )

    def dot(u, v):
        return jnp.sum(u * v, axis=1, keepdims=True)

    shaped = perturbation * occupied
    first, on_atoms, own, of_all = lax.psum(
        (
            times(shaped - SHIFT * start, whole, ((1,), (1,))),
            times(start, beta, ((1,), (1,))),
            times(occupied, pair, ((1,), (1,))),
            times(pair, whole, ((1,), (1,))),
        ),
        "dom",
    )
    own_radial, own_slope = own[:, 0:1], own[:, 1:2]
    first = first + STRENGTH * (own_radial * of_all[1:2] + own_slope * of_all[0:1])
    residual = (
        times(first * (1.0 / total), whole, ((1,), (0,)))
        - STRENGTH * times(on_atoms, beta, ((1,), (0,)))
        - local_part(start)
        - shaped
        - STRENGTH * (own_radial * pair[1:2] + own_slope * pair[0:1])
    )
    correlation, norm = lax.psum((correlate(residual), dot(residual, residual)), "dom")
    image = operator(residual, correlation)
    correlation, curve = lax.psum((correlate(image), dot(residual, image)), "dom")
    alpha = norm / curve
    again = operator(image, correlation)
    later = residual - alpha * image
    later_image = image - alpha * again
    new, bend, cross = lax.psum((dot(later, later), dot(later, later_image), dot(later, image)), "dom")
    ratio = new / norm
    step = new / (bend + ratio * (2.0 * cross + ratio * curve))
    answer = start + alpha * residual + step * (later + ratio * residual)
    return answer, later - step * (later_image + ratio * image)


NT = (((1,), (1,)), ((), ()))
NN = (((1,), (0,)), ((), ()))
MESH = pl.DeviceIdType.MESH


def parts_of(x):
    high = x.astype(jnp.bfloat16)
    return high, (x - high.astype(jnp.float32)).astype(jnp.bfloat16)


def product(a, b, dims):
    def one(u, v):
        return lax.dot_general(u, v, dims, preferred_element_type=jnp.float32)

    return one(a[0], b[0]) + (one(a[0], b[1]) + one(a[1], b[0]))


def fused_kernel(
    atoms,
    slabs,
    occ_in,
    start_in,
    pot,
    pert,
    energy,
    fields,
    answer,
    residual,
    occ,
    start,
    plane_high,
    plane_low,
    whole,
    w_high,
    w_low,
    f_high,
    f_low,
    faces,
    r0,
    w0,
    image,
    part,
    pieces,
    summed,
    totals,
    rows_part,
    rows_in,
    last_part,
    last_in,
    band_send,
    band_recv,
    face_send,
    face_recv,
    hand_send,
    hand_recv,
    sum_send,
    sum_recv,
    all_send,
    all_recv,
    rows_send,
    rows_recv,
    last_send,
    last_recv,
    local_sem,
):
    bands, cells = occ.shape
    every = 4 * bands
    total = cells * slabs
    band = lax.axis_index("band")
    slab = lax.axis_index("dom")
    sibling = band + 1 - 2 * (band % 2)
    across = (band + 2) % 4
    loads = [
        pltpu.make_async_copy(occ_in, occ, local_sem.at[0]),
        pltpu.make_async_copy(start_in, start, local_sem.at[1]),
    ]
    for load in loads:
        load.start()
    barrier = pltpu.get_barrier_semaphore()
    pl.semaphore_signal(barrier, inc=1, device_id={"band": sibling}, device_id_type=MESH)
    pl.semaphore_signal(barrier, inc=1, device_id={"band": across}, device_id_type=MESH)
    peers = [(slab + k) % slabs for k in range(slabs)]
    for k in range(1, slabs):
        pl.semaphore_signal(barrier, inc=1, device_id={"dom": peers[k]}, device_id_type=MESH)
    pl.semaphore_wait(barrier, slabs + 1)

    pending = []

    def send(src, dst, send_sem, recv_sem, device):
        copy = pltpu.make_async_remote_copy(
            src_ref=src,
            dst_ref=dst,
            send_sem=send_sem,
            recv_sem=recv_sem,
            device_id=device,
            device_id_type=MESH,
        )
        copy.start()
        pending.append(copy)
        return copy

    chunk = bands // CHUNKS
    side = slab % 2
    beside = slab + 1 - 2 * side
    beyond = (slab + slabs + 2 - 4 * side) % slabs

    def send_face(turn, field, c):
        return send(
            field.at[pl.ds(c * chunk, chunk)],
            faces.at[turn, side, pl.ds(c * chunk, chunk)],
            face_send.at[turn, c],
            face_recv.at[turn, c],
            {"dom": beside},
        )

    def hand_over(turn, c):
        return send(
            faces.at[turn, 1 - side, pl.ds(c * chunk, chunk)],
            faces.at[turn, side, pl.ds(c * chunk, chunk)],
            hand_send.at[turn, c],
            hand_recv.at[turn, c],
            {"dom": beyond},
        )

    def hand_on(turn, copies, c):
        copies[c].wait_recv()
        copies.append(hand_over(turn, c))

    half = bands // 2
    crossing = [
        send(
            occ_in.at[pl.ds(c * half, half)],
            whole.at[1, pl.ds(c * half, half)],
            band_send.at[c],
            band_recv.at[c],
            {"band": across},
        )
        for c in range(2)
    ]
    to_sibling = send(occ_in, whole.at[0], band_send.at[2], band_recv.at[2], {"band": sibling})
    moving = [send_face(0, start_in, c) for c in range(CHUNKS)]

    def hold(row, block):
        high, low = parts_of(block)
        w_high[row : row + block.shape[0], :] = high
        w_low[row : row + block.shape[0], :] = low

    def hold_field(block):
        high, low = parts_of(block)
        f_high[...] = high
        f_low[...] = low

    def plane_image(field, planes):
        for z in planes:
            cut = slice(z * PLANE, (z + 1) * PLANE)
            image[:, cut] = product(
                (f_high[:, cut], f_low[:, cut]), (plane_high[...], plane_low[...]), NN
            ) + (pot[:, cut] - energy[...]) * field[:, cut]

    def across_planes(turn, field, c):
        def group(i, carry):
            rows = pl.ds(pl.multiple_of(i * 8, 8), 8)
            grid = [
                ref[rows, z * PLANE : (z + 1) * PLANE]
                for ref in (faces.at[turn, 0], field, faces.at[turn, 1])
                for z in range(HALO)
            ]
            for z in range(HALO):
                cut = slice(z * PLANE, (z + 1) * PLANE)
                value = image[rows, cut]
                for d in range(1, 7):
                    value += (-KINETIC * COEF[d]) * (grid[HALO + z - d] + grid[HALO + z + d])
                image[rows, cut] = value
            return carry

        lax.fori_loop(c * chunk // 8, (c + 1) * chunk // 8, group, 0)

    def start_sum(turn):
        return [
            send(
                part.at[turn, pl.ds(pl.multiple_of(peers[k] * 8, 8), 8)],
                pieces.at[turn, k],
                sum_send.at[turn, k],
                sum_recv.at[turn, k],
                {"dom": peers[k]},
            )
            for k in range(1, slabs)
        ]

    def share_sum(turn, copies):
        mine = pl.ds(pl.multiple_of(slab * 8, 8), 8)
        value = part[turn, mine, :]
        for k in range(1, slabs):
            copies[k - 1].wait_recv()
            value += pieces[turn, k]
        summed[turn] = value
        shared = [
            send(
                summed.at[turn],
                totals.at[turn, mine],
                all_send.at[turn, k],
                all_recv.at[turn, k],
                {"dom": peers[k]},
            )
            for k in range(1, slabs)
        ]
        totals[turn, mine, :] = value
        return shared

    def finish_sum(shared):
        for copy in shared:
            copy.wait_recv()

    lane = lax.broadcasted_iota(jnp.int32, (bands, 128), 1)

    def correlate(rows):
        return product((f_high[...], f_low[...]), (w_high[rows, :], w_low[rows, :]), NT)

    def back(coefficients):
        return product(parts_of(coefficients), (w_high[...], w_low[...]), NN)

    one_cell = lax.broadcasted_iota(jnp.int32, (PLANE, PLANE), 0)
    other_cell = lax.broadcasted_iota(jnp.int32, (PLANE, PLANE), 1)
    along_x = (one_cell - other_cell) & (NX - 1)
    along_y = ((one_cell >> 4) - (other_cell >> 4)) & (NY - 1)
    away_x = jnp.minimum(along_x, NX - along_x)
    away_y = jnp.minimum(along_y, NY - along_y)
    away = jnp.where(away_x == 0, away_y, jnp.where(away_y == 0, away_x, NX))
    matrix = jnp.where(away == 0, -KINETIC * 3.0 * COEF[0], 0.0)
    for d in range(1, 7):
        matrix = jnp.where(away == d, -KINETIC * COEF[d], matrix)
    matrix_high, matrix_low = parts_of(matrix.astype(jnp.float32))
    plane_high[...] = matrix_high
    plane_low[...] = matrix_low

    for load in loads:
        load.wait()
    hold(0, occ[...])
    hold(every, fields[...])
    hold_field(start[...])
    plane_image(start, range(HALO))
    hand_on(0, moving, 0)
    hand_on(0, moving, 1)
    ends = slice(every, every + 128)
    on_start = correlate(ends)
    on_own = product(
        (w_high[0:bands, :], w_low[0:bands, :]), (w_high[ends, :], w_low[ends, :]), NT
    )
    part[0, :, every:] = jnp.where(lane < atoms, on_start, on_own)
    hand_on(0, moving, 2)
    shaped = pert[...] * occ[...]
    hold_field(shaped - SHIFT * start[...])
    to_sibling.wait_recv()
    hold(bands, whole[0])
    hand_on(0, moving, 3)
    part[0, :, 0 : 2 * bands] = correlate(slice(0, 2 * bands))
    passed = []
    for c in range(2):
        crossing[c].wait_recv()
        passed.append(
            send(
                whole.at[1, pl.ds(c * half, half)],
                whole.at[2, pl.ds(c * half, half)],
                band_send.at[3 + c],
                band_recv.at[3 + c],
                {"band": sibling},
            )
        )
        hand_on(0, moving, 4 + 2 * c)
        hand_on(0, moving, 5 + 2 * c)
    hold(2 * bands, whole[1])
    for copy in passed:
        copy.wait_recv()
    hold(3 * bands, whole[2])
    part[0, :, 2 * bands : every] = correlate(slice(2 * bands, every))
    copies = start_sum(0)
    pair = slice(every + atoms, every + atoms + 16)
    rows_part[...] = product(
        (w_high[pair, :], w_low[pair, :]), (w_high[0:every, :], w_low[0:every, :]), NT
    )[0:8]
    row_copies = [
        send(rows_part, rows_in.at[k], rows_send.at[k], rows_recv.at[k], {"dom": peers[k]})
        for k in range(1, slabs)
    ]
    shared = share_sum(0, copies)
    for c in range(CHUNKS):
        moving[CHUNKS + c].wait_recv()
        across_planes(0, start, c)
    of_all = rows_part[...]
    for k in range(1, slabs):
        row_copies[k - 1].wait_recv()
        of_all += rows_in[k]
    finish_sum(shared)
    last = totals[0, :, every:]
    own_radial, own_slope = last[:, atoms : atoms + 1], last[:, atoms + 1 : atoms + 2]
    first = totals[0, :, 0:every] + STRENGTH * (own_radial * of_all[1:2] + own_slope * of_all[0:1])
    ends_part = jnp.where(
        lane < atoms,
        last,
        jnp.where(lane == atoms, own_slope, jnp.where(lane == atoms + 1, own_radial, 0.0)),
    )
    r0[...] = (
        back(jnp.concatenate([first * (1.0 / total), -STRENGTH * ends_part], axis=1))
        - image[...]
        - pert[...] * occ[...]
    )

    def apply(turn, field, scalar):
        moving = [send_face(turn, field, c) for c in range(2)]
        hold_field(field[...])
        part[turn, :, 0:every] = correlate(slice(0, every))
        part[turn, :, every:] = jnp.where(lane == atoms, scalar, correlate(ends))
        copies = start_sum(turn)
        face = list(moving)
        handed = []
        for c in range(CHUNKS):
            if c + 2 < CHUNKS:
                face.append(send_face(turn, field, c + 2))
            face[c].wait_recv()
            handed.append(hand_over(turn, c))
            if c < 3:
                plane_image(field, range(2 * c, 2 * c + 2))
            if c == SUM_AT:
                shared = share_sum(turn, copies)
            if c >= 4:
                handed[c - 4].wait_recv()
                across_planes(turn, field, c - 4)
        finish_sum(shared)
        last = totals[turn, :, every:]
        coefficients = jnp.concatenate(
            [
                totals[turn, :, 0:every] * (SHIFT / total),
                jnp.where(lane < atoms, STRENGTH * last, 0.0),
            ],
            axis=1,
        )
        image[...] += back(coefficients)
        for c in range(CHUNKS - 4, CHUNKS):
            handed[c].wait_recv()
            across_planes(turn, field, c)
        return last[:, atoms : atoms + 1]

    def dot(u, v):
        return jnp.sum(u * v, axis=1, keepdims=True)

    norm = apply(1, r0, dot(r0[...], r0[...]))
    w0[...] = image[...]
    curve = apply(2, w0, dot(r0[...], w0[...]))
    alpha = norm / curve
    later = r0[...] - alpha * w0[...]
    later_image = w0[...] - alpha * image[...]
    residual[0] = later
    image[...] = later_image
    three = jnp.where(
        lane == 0,
        dot(later, later),
        jnp.where(
            lane == 1, dot(later, later_image), jnp.where(lane == 2, dot(later, w0[...]), 0.0)
        ),
    )
    eye = jnp.where(
        lax.broadcasted_iota(jnp.int32, (128, 128), 0)
        == lax.broadcasted_iota(jnp.int32, (128, 128), 1),
        1.0,
        0.0,
    ).astype(jnp.float32)
    three = jnp.concatenate([three, jnp.zeros((128 - bands, 128), jnp.float32)], axis=0)
    last_part[...] = lax.dot_general(
        eye[0:8], three, NT, precision=HIGH, preferred_element_type=jnp.float32
    )
    last_copies = [
        send(last_part, last_in.at[k], last_send.at[k], last_recv.at[k], {"dom": peers[k]})
        for k in range(1, slabs)
    ]
    value = last_part[...]
    for k in range(1, slabs):
        last_copies[k - 1].wait_recv()
        value += last_in[k]
    three = lax.dot_general(
        eye[0:bands], value, NT, precision=HIGH, preferred_element_type=jnp.float32
    )
    new, bend, cross = three[:, 0:1], three[:, 1:2], three[:, 2:3]
    ratio = new / norm
    step = new / (bend + ratio * (2.0 * cross + ratio * curve))
    later = residual[0]
    answer[0] = start[...] + alpha * r0[...] + step * (later + ratio * r0[...])
    residual[0] = later - step * (image[...] + ratio * w0[...])
    for copy in pending:
        copy.wait_send()


def fused(atoms, occupied, start_guess, potential, perturbation, energy, fields):
    slabs = lax.axis_size("dom")
    bands, cells = occupied.shape
    every = 4 * bands
    rows = every + 128
    f32, bf16 = jnp.float32, jnp.bfloat16
    vmem = pl.BlockSpec(memory_space=pltpu.VMEM)
    out = jax.ShapeDtypeStruct((1, bands, cells), f32)
    dma = pltpu.SemaphoreType.DMA
    field = pltpu.VMEM((bands, cells), f32)
    return pl.pallas_call(
        functools.partial(fused_kernel, atoms, slabs),
        out_shape=(out, out),
        in_specs=[pl.BlockSpec(memory_space=pl.ANY)] * 2 + [vmem] * 4,
        out_specs=(vmem, vmem),
        scratch_shapes=[
            field,
            field,
            pltpu.VMEM((PLANE, PLANE), bf16),
            pltpu.VMEM((PLANE, PLANE), bf16),
            pltpu.VMEM((3, bands, cells), f32),
            pltpu.VMEM((rows, cells), bf16),
            pltpu.VMEM((rows, cells), bf16),
            pltpu.VMEM((bands, cells), bf16),
            pltpu.VMEM((bands, cells), bf16),
            pltpu.VMEM((3, 2, bands, cells), f32),
            field,
            field,
            field,
            pltpu.VMEM((3, bands, rows), f32),
            pltpu.VMEM((3, slabs, 8, rows), f32),
            pltpu.VMEM((3, 8, rows), f32),
            pltpu.VMEM((3, bands, rows), f32),
            pltpu.VMEM((8, every), f32),
            pltpu.VMEM((slabs, 8, every), f32),
            pltpu.VMEM((8, 128), f32),
            pltpu.VMEM((slabs, 8, 128), f32),
            dma((5,)),
            dma((5,)),
            dma((3, CHUNKS)),
            dma((3, CHUNKS)),
            dma((3, CHUNKS)),
            dma((3, CHUNKS)),
            dma((3, slabs)),
            dma((3, slabs)),
            dma((3, slabs)),
            dma((3, slabs)),
            dma((slabs,)),
            dma((slabs,)),
            dma((slabs,)),
            dma((slabs,)),
            dma((2,)),
        ],
        compiler_params=pltpu.CompilerParams(
            collective_id=0, has_side_effects=True, vmem_limit_bytes=40 * 1024 * 1024
        ),
    )(
        occupied,
        start_guess[0],
        potential,
        perturbation,
        energy,
        fields,
    )


def local(
    occupied,
    start_guess,
    potential,
    perturbation,
    band_energy,
    beta_radial,
    beta_slope,
    atom_owner,
    atom_site,
    sphere_offset,
    displaced,
):
    slabs = lax.axis_size("dom")
    bands, cells = start_guess.shape[1:]
    atoms = atom_owner.shape[0]
    fields = atom_fields(
        slabs, cells, beta_radial, beta_slope, sphere_offset, atom_owner, atom_site, displaced
    )
    fits = bands == 8 * slabs and lax.axis_size("band") == 4 and atoms % 16 == 0 and atoms <= 112
    if fits and cells == HALO * PLANE:
        return fused(
            atoms,
            occupied,
            start_guess,
            potential[None, :],
            perturbation,
            band_energy[:, None],
            fields,
        )
    answer, residual = plain(
        occupied,
        start_guess[0],
        potential[None, :],
        perturbation,
        band_energy[:, None],
        fields[:atoms],
        fields[atoms : atoms + 8],
        jnp.asarray(plane_matrix()),
    )
    return answer[None], residual[None]


def solution(mesh):
    return jax.shard_map(
        local,
        mesh=mesh,
        in_specs=(
            P("band", "dom"),
            P(None, "band", "dom"),
            P("dom"),
            P(None, "dom"),
            P("band"),
            P(),
            P(),
            P(),
            P(),
            P(),
            P(),
        ),
        out_specs=(P(None, "band", "dom"), P(None, "band", "dom")),
        check_vma=False,
    )
```

profile of v0, /device:TPU:0, one launch (start us, length us, event | category | flops | bytes accessed | tf_op | source)
XLA Modules:
  0.0 75.8 jit_solution(11207360278248796868)
XLA Ops:
  0.6 0.0 copy-start.8
  1.3 0.0 copy-done.8
  1.3 0.0 copy-start.9
  1.3 0.6 copy-done.9
  2.0 0.0 copy-start.2
  2.0 0.0 copy-start.4
  2.0 0.0 copy-start.5
  2.0 0.0 copy-start.6
  2.0 0.0 copy-start.7
  2.0 0.1 copy.13.energy
  2.1 0.6 copy-done.2
  2.7 0.0 copy-done.4
  2.7 0.0 copy-done.5
  2.7 0.0 copy-done.6
  2.7 0.0 copy-done.7
  2.7 0.0 copy-start
  2.7 0.0 copy-start.1
  2.7 0.0 copy-start.3
  2.7 1.7 %shard_map.122.fields = f32[128,1536]{1,0:T(8,128)S(1)} custom-call(f32[1,512]{1,0:T(1,128)S(1)} %bitcast.5, f32[1,512]{1,0:T(1,128)S(1)} %bitcast.6, s32[3,512]{1,0:T(4,128)S(1)} %copy-done.2, s32[32]{0:T(128)S(1)} %copy-done.7, s32[3,32]{1,0:T(4,128)S(1)} %copy-done.6, s32[1]{0:T(128)S(6)} %copy.16.displaced), custom_call_target="tpu_custom_call" | custom-call | tf_op jit(solution)/shard_map/pallas_call | solution.py:92
  4.5 0.0 copy-done
  4.5 0.0 copy-done.1
  4.5 0.0 copy-done.3
  4.5 69.8 %shard_map.123 = (f32[1,64,1536]{2,1,0:T(8,128)S(1)}, f32[1,64,1536]{2,1,0:T(8,128)S(1)}) custom-call(f32[64,1536]{1,0:T(8,128)S(1)} %copy-done, f32[64,1536]{1,0:T(8,128)S(1)} %bitcast.4, f32[1,1536]{1,0:T(1,128)S(1)} %broadcast_in_dim.12.pot, f32[1,1536]{1,0:T(1,128)S(1)} %copy-done.3, f32[64,1]{1,0:T(8,128)S(1)} %copy.13.energy, ...), custom_call_target="tpu_custom_call" | custom-call | tf_op jit(solution)/shard_map/pallas_call | solution.py:576
  74.3 0.7 copy.17
  75.1 0.7 copy.18
  (1 shorter events, 0.0 us)
Async XLA Ops:
  0.6 0.7 copy-start.8
  1.3 0.7 copy-start.9
  2.0 0.7 copy-start.2
  2.0 0.7 copy-start.4
  2.0 0.7 copy-start.5
  2.0 0.7 copy-start.6
  2.0 0.7 copy-start.7
  2.7 1.8 %copy-start = (f32[64,1536]{1,0:T(8,128)S(1)}, f32[64,1536]{1,0:T(8,128)}, u32[]{:S(2)}) copy-start(f32[64,1536]{1,0:T(8,128)} %occ_in.1) | copy-start | bytes 1179652
  2.7 1.8 %copy-start.1 = (f32[1,64,1536]{2,1,0:T(8,128)S(1)}, f32[1,64,1536]{2,1,0:T(8,128)}, u32[]{:S(2)}) copy-start(f32[1,64,1536]{2,1,0:T(8,128)} %param.12) | copy-start | bytes 1179652
  2.7 1.8 %copy-start.3 = (f32[1,1536]{1,0:T(1,128)S(1)}, f32[1,1536]{1,0:T(1,128)}, u32[]{:S(2)}) copy-start(f32[1,1536]{1,0:T(1,128)} %pert.1) | copy-start | bytes 18436
where the time goes:
time: 76.1 us; the launch traced here: 75.8 us
  Pallas kernels  71.6 us (94%)
  local copies, waits for them, and re-layouts  2.91 us (4%)
  between operations  1.35 us (2%)
    pallas_call x1, Pallas kernels, fused(): pl.pallas_call(functools.partial(fused_kernel, atoms, slabs), out_shape=(...  69.8 us
    unnamed x22, local copies, waits for them, and re-layouts  2.81 us
    pallas_call x1, Pallas kernels, atom_fields(): pl.pallas_call(functools.partial(fields_kernel, slabs, depth), out_shape=...  1.75 us

commit v1 on v0

--- a/solution.py
+++ b/solution.py
@@ -13,6 +13,7 @@
 HALO = 6
 CHUNKS = 8
 SUM_AT = 3
+FINISH = 4
 RAD = 5
 
 COEF = (
@@ -84,6 +85,61 @@
             out[row : row + 1, z * PLANE : (z + 1) * PLANE] = field[z : z + 1]
 
 
+def place_fields(slab, slabs, depth, atoms, radial, slope, offset, owner, site, displaced, fields):
+    planes = slabs * depth
+    points = offset.shape[1]
+    count = atoms + 8
+    rows = lax.broadcasted_iota(jnp.int32, (16, points), 0)
+    along_z = rows == offset[0:1, :] + RAD
+    in_plane = (offset[1:2, :] & (NY - 1)) * NX + (offset[2:3, :] & (NX - 1))
+    hot = jnp.where(
+        lax.broadcasted_iota(jnp.int32, (PLANE, points), 0) == in_plane, 1.0, 0.0
+    ).astype(jnp.float32)
+    left = jnp.concatenate(
+        [jnp.where(along_z, radial[...], 0.0), jnp.where(along_z, slope[...], 0.0)], axis=0
+    )
+    template = lax.dot_general(
+        left, hot, (((1,), (1,)), ((), ())), precision=HIGH, preferred_element_type=jnp.float32
+    )
+    row = lax.broadcasted_iota(jnp.int32, (count, atoms), 0)
+    atom = lax.broadcasted_iota(jnp.int32, (count, atoms), 1)
+    chosen = atom == jnp.where(row < atoms, row, displaced[0])
+
+    def column(values):
+        return jnp.sum(jnp.where(chosen, values, 0), axis=1, keepdims=True)
+
+    centre = column(owner[...]) * depth + column(site[0:1, :])
+    turn_y, turn_x = column(site[1:2, :]), column(site[2:3, :])
+    row = lax.broadcasted_iota(jnp.int32, (count, 32), 0)
+    lane = lax.broadcasted_iota(jnp.int32, (count, 32), 1)
+    picks = []
+    for z in range(depth):
+        at = slab * depth + (z + RAD) - centre
+        at = jnp.where(at < 0, at + planes, jnp.where(at >= planes, at - planes, at))
+        at = jnp.where(at < 16, at, -32)
+        pick = lane == at + jnp.where(row == atoms + 1, 16, 0)
+        picks.append(jnp.where(pick & (row < atoms + 2), 1.0, 0.0).astype(jnp.float32))
+    value = lax.dot_general(
+        jnp.concatenate(picks, axis=0),
+        template,
+        (((1,), (0,)), ((), ())),
+        precision=HIGH,
+        preferred_element_type=jnp.float32,
+    )
+    x = lax.broadcasted_iota(jnp.int32, (count, PLANE), 1) & (NX - 1)
+    wide_x = jnp.broadcast_to(turn_x, (count, PLANE))
+    wide_y = jnp.broadcast_to(turn_y, (count, PLANE))
+    fields[atoms:, :] = jnp.zeros((fields.shape[0] - atoms, fields.shape[1]), jnp.float32)
+    for z in range(depth):
+        block = value[z * count : (z + 1) * count]
+        for d in (1, 2, 4, 8):
+            near, far = pltpu.roll(block, d, 1), pltpu.roll(block, PLANE + d - NX, 1)
+            block = jnp.where((wide_x & d) != 0, jnp.where(x >= d, near, far), block)
+        for d in (1, 2, 4, 8):
+            block = jnp.where((wide_y & d) != 0, pltpu.roll(block, d * NX, 1), block)
+        fields[0:count, z * PLANE : (z + 1) * PLANE] = block
+
+
 def atom_fields(slabs, cells, beta_radial, beta_slope, offset, owner, site, displaced):
     atoms = owner.shape[0]
     depth = cells // PLANE
@@ -194,14 +250,31 @@
     slabs,
     occ_in,
     start_in,
+    pot_in,
+    pert_in,
+    energy_in,
+    radial_in,
+    slope_in,
+    offset_in,
+    owner_in,
+    site_in,
+    displaced,
+    start,
+    r0,
+    w0,
+    image,
+    weights,
+    occ,
     pot,
     pert,
+    energy_row,
+    radial,
+    slope,
+    offset,
+    owner,
+    site,
     energy,
     fields,
-    answer,
-    residual,
-    occ,
-    start,
     plane_high,
     plane_low,
     whole,
@@ -210,9 +283,6 @@
     f_high,
     f_low,
     faces,
-    r0,
-    w0,
-    image,
     part,
     pieces,
     summed,
@@ -244,18 +314,31 @@
     slab = lax.axis_index("dom")
     sibling = band + 1 - 2 * (band % 2)
     across = (band + 2) % 4
-    loads = [
-        pltpu.make_async_copy(occ_in, occ, local_sem.at[0]),
-        pltpu.make_async_copy(start_in, start, local_sem.at[1]),
-    ]
-    for load in loads:
-        load.start()
     barrier = pltpu.get_barrier_semaphore()
     pl.semaphore_signal(barrier, inc=1, device_id={"band": sibling}, device_id_type=MESH)
     pl.semaphore_signal(barrier, inc=1, device_id={"band": across}, device_id_type=MESH)
     peers = [(slab + k) % slabs for k in range(slabs)]
     for k in range(1, slabs):
         pl.semaphore_signal(barrier, inc=1, device_id={"dom": peers[k]}, device_id_type=MESH)
+    loads = [
+        pltpu.make_async_copy(src, dst, local_sem.at[i])
+        for i, (src, dst) in enumerate(
+            (
+                (offset_in, offset),
+                (radial_in, radial),
+                (slope_in, slope),
+                (owner_in, owner),
+                (site_in, site),
+                (energy_in, energy_row),
+                (pot_in, pot),
+                (pert_in, pert),
+                (start_in, start),
+                (occ_in, occ),
+            )
+        )
+    ]
+    for load in loads:
+        load.start()
     pl.semaphore_wait(barrier, slabs + 1)
 
     pending = []
@@ -327,9 +410,12 @@
     def plane_image(field, planes):
         for z in planes:
             cut = slice(z * PLANE, (z + 1) * PLANE)
+            local_pot = jnp.concatenate(
+                [pot[i : i + 1] for i in range(z * PLANE // 128, (z + 1) * PLANE // 128)], axis=1
+            )
             image[:, cut] = product(
                 (f_high[:, cut], f_low[:, cut]), (plane_high[...], plane_low[...]), NN
-            ) + (pot[:, cut] - energy[...]) * field[:, cut]
+            ) + (local_pot - energy[:, 0:1]) * field[:, cut]
 
     def across_planes(turn, field, c):
         def group(i, carry):
@@ -407,7 +493,17 @@
     plane_high[...] = matrix_high
     plane_low[...] = matrix_low
 
-    for load in loads:
+    for load in loads[:8]:
+        load.wait()
+    rows = lax.broadcasted_iota(jnp.int32, (bands, bands), 0)
+    columns = lax.broadcasted_iota(jnp.int32, (bands, bands), 1)
+    energy[...] = jnp.broadcast_to(
+        jnp.sum(jnp.where(rows == columns, energy_row[...], 0.0), axis=1, keepdims=True), (bands, 128)
+    )
+    place_fields(
+        slab, slabs, cells // PLANE, atoms, radial, slope, offset, owner, site, displaced, fields
+    )
+    for load in loads[8:]:
         load.wait()
     hold(0, occ[...])
     hold(every, fields[...])
@@ -480,20 +576,17 @@
     )
 
     def apply(turn, field, scalar):
-        moving = [send_face(turn, field, c) for c in range(2)]
+        face = [send_face(turn, field, c) for c in range(2)]
         hold_field(field[...])
         part[turn, :, 0:every] = correlate(slice(0, every))
         part[turn, :, every:] = jnp.where(lane == atoms, scalar, correlate(ends))
         copies = start_sum(turn)
-        face = list(moving)
+        face += [send_face(turn, field, c) for c in range(2, CHUNKS)]
+        plane_image(field, range(HALO))
         handed = []
         for c in range(CHUNKS):
-            if c + 2 < CHUNKS:
-                face.append(send_face(turn, field, c + 2))
             face[c].wait_recv()
             handed.append(hand_over(turn, c))
-            if c < 3:
-                plane_image(field, range(2 * c, 2 * c + 2))
             if c == SUM_AT:
                 shared = share_sum(turn, copies)
             if c >= 4:
@@ -523,8 +616,6 @@
     alpha = norm / curve
     later = r0[...] - alpha * w0[...]
     later_image = w0[...] - alpha * image[...]
-    residual[0] = later
-    image[...] = later_image
     three = jnp.where(
         lane == 0,
         dot(later, later),
@@ -556,31 +647,71 @@
     new, bend, cross = three[:, 0:1], three[:, 1:2], three[:, 2:3]
     ratio = new / norm
     step = new / (bend + ratio * (2.0 * cross + ratio * curve))
-    later = residual[0]
-    answer[0] = start[...] + alpha * r0[...] + step * (later + ratio * r0[...])
-    residual[0] = later - step * (image[...] + ratio * w0[...])
+    weights[...] = jnp.where(
+        lane == 0, alpha + step * (1.0 + ratio), jnp.where(lane == 1, step * alpha, 0.0)
+    )
     for copy in pending:
         copy.wait_send()
 
 
-def fused(atoms, occupied, start_guess, potential, perturbation, energy, fields):
+def finish_kernel(start, r0, w0, z0, weights, answer, residual, held, sems):
+    bands = start.shape[0]
+    size = bands // FINISH
+    copies = []
+    for c in range(FINISH):
+        rows = pl.ds(c * size, size)
+        first, second = weights[rows, 0:1], weights[rows, 1:2]
+        held[0, rows] = start[rows] + first * r0[rows] - second * w0[rows]
+        held[1, rows] = r0[rows] - first * w0[rows] + second * z0[rows]
+        for i, out in enumerate((answer, residual)):
+            copy = pltpu.make_async_copy(held.at[i, rows], out.at[0, rows], sems.at[i, c])
+            copy.start()
+            copies.append(copy)
+    for copy in copies:
+        copy.wait()
+
+
+def fused(
+    occupied,
+    start_guess,
+    potential,
+    perturbation,
+    energy,
+    beta_radial,
+    beta_slope,
+    offset,
+    owner,
+    site,
+    displaced,
+):
     slabs = lax.axis_size("dom")
+    atoms = owner.shape[0]
     bands, cells = occupied.shape
     every = 4 * bands
     rows = every + 128
-    f32, bf16 = jnp.float32, jnp.bfloat16
+    f32, bf16, i32 = jnp.float32, jnp.bfloat16, jnp.int32
     vmem = pl.BlockSpec(memory_space=pltpu.VMEM)
-    out = jax.ShapeDtypeStruct((1, bands, cells), f32)
+    hbm = pl.BlockSpec(memory_space=pltpu.HBM)
+    out = jax.ShapeDtypeStruct((bands, cells), f32)
     dma = pltpu.SemaphoreType.DMA
-    field = pltpu.VMEM((bands, cells), f32)
-    return pl.pallas_call(
+    points = offset.shape[1]
+    state = pl.pallas_call(
         functools.partial(fused_kernel, atoms, slabs),
-        out_shape=(out, out),
-        in_specs=[pl.BlockSpec(memory_space=pl.ANY)] * 2 + [vmem] * 4,
-        out_specs=(vmem, vmem),
+        out_shape=(out, out, out, out, jax.ShapeDtypeStruct((bands, 128), f32)),
+        in_specs=[hbm] * 10 + [pl.BlockSpec(memory_space=pltpu.SMEM)],
+        out_specs=(vmem,) * 5,
         scratch_shapes=[
-            field,
-            field,
+            pltpu.VMEM((bands, cells), f32),
+            pltpu.VMEM((cells // 128, 128), f32),
+            pltpu.VMEM((1, cells), f32),
+            pltpu.VMEM((1, bands), f32),
+            pltpu.VMEM((1, points), f32),
+            pltpu.VMEM((1, points), f32),
+            pltpu.VMEM((3, points), i32),
+            pltpu.VMEM((1, atoms), i32),
+            pltpu.VMEM((3, atoms), i32),
+            pltpu.VMEM((bands, 128), f32),
+            pltpu.VMEM((128, cells), f32),
             pltpu.VMEM((PLANE, PLANE), bf16),
             pltpu.VMEM((PLANE, PLANE), bf16),
             pltpu.VMEM((3, bands, cells), f32),
@@ -589,9 +720,6 @@
             pltpu.VMEM((bands, cells), bf16),
             pltpu.VMEM((bands, cells), bf16),
             pltpu.VMEM((3, 2, bands, cells), f32),
-            field,
-            field,
-            field,
             pltpu.VMEM((3, bands, rows), f32),
             pltpu.VMEM((3, slabs, 8, rows), f32),
             pltpu.VMEM((3, 8, rows), f32),
@@ -614,19 +742,38 @@
             dma((slabs,)),
             dma((slabs,)),
             dma((slabs,)),
-            dma((2,)),
+            dma((10,)),
         ],
         compiler_params=pltpu.CompilerParams(
             collective_id=0, has_side_effects=True, vmem_limit_bytes=40 * 1024 * 1024
         ),
     )(
-        occupied,
-        start_guess[0],
-        potential,
-        perturbation,
-        energy,
-        fields,
-    )
+        *(
+            pltpu.with_memory_space_constraint(x, pltpu.HBM)
+            for x in (
+                occupied,
+                start_guess[0],
+                potential.reshape(cells // 128, 128),
+                perturbation,
+                energy[None, :],
+                beta_radial[None, :],
+                beta_slope[None, :],
+                offset,
+                owner[None, :],
+                site,
+            )
+        ),
+        displaced,
+    )
+    final = jax.ShapeDtypeStruct((1, bands, cells), f32)
+    return pl.pallas_call(
+        finish_kernel,
+        out_shape=(final, final),
+        in_specs=[vmem] * 5,
+        out_specs=(hbm, hbm),
+        scratch_shapes=[pltpu.VMEM((2, bands, cells), f32), dma((2, FINISH))],
+        compiler_params=pltpu.CompilerParams(vmem_limit_bytes=16 * 1024 * 1024),
+    )(*state)
 
 
 def local(
@@ -645,20 +792,24 @@
     slabs = lax.axis_size("dom")
     bands, cells = start_guess.shape[1:]
     atoms = atom_owner.shape[0]
-    fields = atom_fields(
-        slabs, cells, beta_radial, beta_slope, sphere_offset, atom_owner, atom_site, displaced
-    )
     fits = bands == 8 * slabs and lax.axis_size("band") == 4 and atoms % 16 == 0 and atoms <= 112
     if fits and cells == HALO * PLANE:
         return fused(
-            atoms,
             occupied,
             start_guess,
-            potential[None, :],
+            potential,
             perturbation,
-            band_energy[:, None],
-            fields,
-        )
+            band_energy,
+            beta_radial,
+            beta_slope,
+            sphere_offset,
+            atom_owner,
+            atom_site,
+            displaced,
+        )
+    fields = atom_fields(
+        slabs, cells, beta_radial, beta_slope, sphere_offset, atom_owner, atom_site, displaced
+    )
     answer, residual = plain(
         occupied,
         start_guess[0],

time: 76.1 us -> 72.5 us (0.953)
  local copies, waits for them, and re-layouts: 2.91 us -> 0 us
    unnamed x22 -> x0, local copies, waits for them, and re-layouts: 2.81 us -> none
where the time goes in v1:
time: 72.5 us; the launch traced here: 72.3 us
  Pallas kernels  71 us (98%)
  between operations  1.29 us (2%)
    pallas_call x1, Pallas kernels, fused(): pl.pallas_call(functools.partial(fused_kernel, atoms, slabs), out_shape=(...  70 us

profile of v1, /device:TPU:0, one launch (start us, length us, event | category | flops | bytes accessed | tf_op | source)
XLA Modules:
  0.0 72.3 jit_solution(12827803495933621448)
XLA Ops:
  1.3 70.0 %shard_map.122 = (f32[64,1536]{1,0:T(8,128)S(1)}, f32[64,1536]{1,0:T(8,128)S(1)}, f32[64,1536]{1,0:T(8,128)S(1)}, f32[64,1536]{1,0:T(8,128)S(1)}, f32[64,128]{1,0:T(8,128)S(1)}) custom-call(f32[64,1536]{1,0:T(8,128)} %occ_in.1, f32[64,1536]{1,0:T(8,128)} %bitcast.6, f32[12,128]{1,0:T(8,128)} %bitcast.7, f32[1,1536]{1,0:T(1,128)} %pert_in.1, ...), custom_call_target="tpu_custom_call" | custom-call | tf_op jit(solution)/shard_map/pallas_call | solution.py:698
  71.2 1.1 %shard_map.123 = (f32[1,64,1536]{2,1,0:T(8,128)}, f32[1,64,1536]{2,1,0:T(8,128)}) custom-call(f32[64,1536]{1,0:T(8,128)S(1)} %get-tuple-element.7.start, f32[64,1536]{1,0:T(8,128)S(1)} %get-tuple-element.8.r0, f32[64,1536]{1,0:T(8,128)S(1)} %get-tuple-element.9.w0, f32[64,1536]{1,0:T(8,128)S(1)} %get-tuple-element.10.z0, f32[64,128]{1,0:T(8,128)S(1)} %get-tuple-element.11.weights), custom_call_target="tpu_custom_call" | custom-call | tf_op jit(solution)/shard_map/pallas_call | solution.py:769

commit v2 on v1

--- a/solution.py
+++ b/solution.py
@@ -12,8 +12,11 @@
 PLANE = NY * NX
 HALO = 6
 CHUNKS = 8
-SUM_AT = 3
+SUM_AT = 1
 FINISH = 4
+PIECES = 4
+EAGER = 0
+DEPTH = 3
 RAD = 5
 
 COEF = (
@@ -287,8 +290,6 @@
     pieces,
     summed,
     totals,
-    rows_part,
-    rows_in,
     last_part,
     last_in,
     band_send,
@@ -301,8 +302,6 @@
     sum_recv,
     all_send,
     all_recv,
-    rows_send,
-    rows_recv,
     last_send,
     last_recv,
     local_sem,
@@ -343,7 +342,7 @@
 
     pending = []
 
-    def send(src, dst, send_sem, recv_sem, device):
+    def send(src, dst, send_sem, recv_sem, device, begin=True):
         copy = pltpu.make_async_remote_copy(
             src_ref=src,
             dst_ref=dst,
@@ -352,7 +351,8 @@
             device_id=device,
             device_id_type=MESH,
         )
-        copy.start()
+        if begin:
+            copy.start()
         pending.append(copy)
         return copy
 
@@ -361,13 +361,14 @@
     beside = slab + 1 - 2 * side
     beyond = (slab + slabs + 2 - 4 * side) % slabs
 
-    def send_face(turn, field, c):
+    def send_face(turn, field, c, begin=True):
         return send(
             field.at[pl.ds(c * chunk, chunk)],
             faces.at[turn, side, pl.ds(c * chunk, chunk)],
             face_send.at[turn, c],
             face_recv.at[turn, c],
             {"dom": beside},
+            begin,
         )
 
     def hand_over(turn, c):
@@ -383,7 +384,7 @@
         copies[c].wait_recv()
         copies.append(hand_over(turn, c))
 
-    half = bands // 2
+    half = bands // PIECES
     crossing = [
         send(
             occ_in.at[pl.ds(c * half, half)],
@@ -392,9 +393,9 @@
             band_recv.at[c],
             {"band": across},
         )
-        for c in range(2)
+        for c in range(PIECES)
     ]
-    to_sibling = send(occ_in, whole.at[0], band_send.at[2], band_recv.at[2], {"band": sibling})
+    to_sibling = send(occ_in, whole.at[0], band_send.at[2 * PIECES], band_recv.at[2 * PIECES], {"band": sibling})
     moving = [send_face(0, start_in, c) for c in range(CHUNKS)]
 
     def hold(row, block):
@@ -479,6 +480,18 @@
     def back(coefficients):
         return product(parts_of(coefficients), (w_high[...], w_low[...]), NN)
 
+    pair = slice(every, every + 128)
+
+    def pair_part(q, block):
+        rows = slice(q * bands, (q + 1) * bands)
+        mine = product(
+            (w_high[rows, :], w_low[rows, :]), (w_high[pair, :], w_low[pair, :]), NT
+        )
+        if q:
+            mine = pltpu.roll(mine, 2 * q, 1)
+        at = atoms + 2 * q
+        return jnp.where((lane == at) | (lane == at + 1), mine, block)
+
     one_cell = lax.broadcasted_iota(jnp.int32, (PLANE, PLANE), 0)
     other_cell = lax.broadcasted_iota(jnp.int32, (PLANE, PLANE), 1)
     along_x = (one_cell - other_cell) & (NX - 1)
@@ -513,10 +526,6 @@
     hand_on(0, moving, 1)
     ends = slice(every, every + 128)
     on_start = correlate(ends)
-    on_own = product(
-        (w_high[0:bands, :], w_low[0:bands, :]), (w_high[ends, :], w_low[ends, :]), NT
-    )
-    part[0, :, every:] = jnp.where(lane < atoms, on_start, on_own)
     hand_on(0, moving, 2)
     shaped = pert[...] * occ[...]
     hold_field(shaped - SHIFT * start[...])
@@ -524,75 +533,90 @@
     hold(bands, whole[0])
     hand_on(0, moving, 3)
     part[0, :, 0 : 2 * bands] = correlate(slice(0, 2 * bands))
+    on_fields = pair_part(0, pair_part(1, on_start))
     passed = []
-    for c in range(2):
+    for c in range(PIECES):
         crossing[c].wait_recv()
         passed.append(
             send(
                 whole.at[1, pl.ds(c * half, half)],
                 whole.at[2, pl.ds(c * half, half)],
-                band_send.at[3 + c],
-                band_recv.at[3 + c],
+                band_send.at[PIECES + c],
+                band_recv.at[PIECES + c],
                 {"band": sibling},
             )
         )
-        hand_on(0, moving, 4 + 2 * c)
-        hand_on(0, moving, 5 + 2 * c)
-    hold(2 * bands, whole[1])
-    for copy in passed:
-        copy.wait_recv()
-    hold(3 * bands, whole[2])
+        hand_on(0, moving, 4 + c)
+        hold(2 * bands + c * half, whole[1, c * half : (c + 1) * half])
+        if c > 0:
+            passed[c - 1].wait_recv()
+            hold(3 * bands + (c - 1) * half, whole[2, (c - 1) * half : c * half])
+    passed[PIECES - 1].wait_recv()
+    hold(4 * bands - half, whole[2, bands - half :])
     part[0, :, 2 * bands : every] = correlate(slice(2 * bands, every))
+    part[0, :, every:] = pair_part(2, pair_part(3, on_fields))
     copies = start_sum(0)
-    pair = slice(every + atoms, every + atoms + 16)
-    rows_part[...] = product(
-        (w_high[pair, :], w_low[pair, :]), (w_high[0:every, :], w_low[0:every, :]), NT
-    )[0:8]
-    row_copies = [
-        send(rows_part, rows_in.at[k], rows_send.at[k], rows_recv.at[k], {"dom": peers[k]})
-        for k in range(1, slabs)
-    ]
     shared = share_sum(0, copies)
     for c in range(CHUNKS):
         moving[CHUNKS + c].wait_recv()
         across_planes(0, start, c)
-    of_all = rows_part[...]
-    for k in range(1, slabs):
-        row_copies[k - 1].wait_recv()
-        of_all += rows_in[k]
     finish_sum(shared)
     last = totals[0, :, every:]
     own_radial, own_slope = last[:, atoms : atoms + 1], last[:, atoms + 1 : atoms + 2]
-    first = totals[0, :, 0:every] + STRENGTH * (own_radial * of_all[1:2] + own_slope * of_all[0:1])
-    ends_part = jnp.where(
-        lane < atoms,
-        last,
-        jnp.where(lane == atoms, own_slope, jnp.where(lane == atoms + 1, own_radial, 0.0)),
-    )
+    swapped = jnp.where(
+        lane == atoms, own_slope, jnp.where(lane == atoms + 1, own_radial, 0.0)
+    )
+    of_all = jnp.concatenate(
+        [last] + [pltpu.roll(last, 128 - 2 * q, 1) for q in range(1, 4)], axis=0
+    )
+    first = totals[0, :, 0:every] + STRENGTH * product(parts_of(swapped), parts_of(of_all), NT)
+    ends_part = jnp.where(lane < atoms, last, swapped)
     r0[...] = (
         back(jnp.concatenate([first * (1.0 / total), -STRENGTH * ends_part], axis=1))
         - image[...]
         - pert[...] * occ[...]
     )
 
-    def apply(turn, field, scalar):
+    def apply(turn, field, scalar, between=None):
         face = [send_face(turn, field, c) for c in range(2)]
         hold_field(field[...])
         part[turn, :, 0:every] = correlate(slice(0, every))
         part[turn, :, every:] = jnp.where(lane == atoms, scalar, correlate(ends))
         copies = start_sum(turn)
-        face += [send_face(turn, field, c) for c in range(2, CHUNKS)]
+        face += [send_face(turn, field, c, False) for c in range(2, CHUNKS)]
+
+        @pl.when(band % 2 == EAGER)
+        def _():
+            for copy in face[2:]:
+                copy.start()
+
+        @pl.when(band % 2 != EAGER)
+        def _():
+            for copy in face[2:DEPTH]:
+                copy.start()
+
         plane_image(field, range(HALO))
         handed = []
         for c in range(CHUNKS):
             face[c].wait_recv()
             handed.append(hand_over(turn, c))
+            if c + DEPTH < CHUNKS:
+
+                @pl.when(band % 2 != EAGER)
+                def _():
+                    face[c + DEPTH].start()
+
             if c == SUM_AT:
                 shared = share_sum(turn, copies)
             if c >= 4:
                 handed[c - 4].wait_recv()
                 across_planes(turn, field, c - 4)
         finish_sum(shared)
+        if between is not None:
+            for c in range(CHUNKS - 4, CHUNKS):
+                handed[c].wait_recv()
+                across_planes(turn, field, c)
+            between(totals[turn, :, every + atoms : every + atoms + 1])
         last = totals[turn, :, every:]
         coefficients = jnp.concatenate(
             [
@@ -602,41 +626,49 @@
             axis=1,
         )
         image[...] += back(coefficients)
-        for c in range(CHUNKS - 4, CHUNKS):
-            handed[c].wait_recv()
-            across_planes(turn, field, c)
-        return last[:, atoms : atoms + 1]
+        if between is None:
+            for c in range(CHUNKS - 4, CHUNKS):
+                handed[c].wait_recv()
+                across_planes(turn, field, c)
+        return last[:, atoms : atoms + 1], coefficients
 
     def dot(u, v):
         return jnp.sum(u * v, axis=1, keepdims=True)
 
-    norm = apply(1, r0, dot(r0[...], r0[...]))
+    norm, _ = apply(1, r0, dot(r0[...], r0[...]))
     w0[...] = image[...]
-    curve = apply(2, w0, dot(r0[...], w0[...]))
-    alpha = norm / curve
-    later = r0[...] - alpha * w0[...]
-    later_image = w0[...] - alpha * image[...]
-    three = jnp.where(
-        lane == 0,
-        dot(later, later),
-        jnp.where(
-            lane == 1, dot(later, later_image), jnp.where(lane == 2, dot(later, w0[...]), 0.0)
-        ),
-    )
     eye = jnp.where(
         lax.broadcasted_iota(jnp.int32, (128, 128), 0)
         == lax.broadcasted_iota(jnp.int32, (128, 128), 1),
         1.0,
         0.0,
     ).astype(jnp.float32)
-    three = jnp.concatenate([three, jnp.zeros((128 - bands, 128), jnp.float32)], axis=0)
-    last_part[...] = lax.dot_general(
-        eye[0:8], three, NT, precision=HIGH, preferred_element_type=jnp.float32
-    )
-    last_copies = [
-        send(last_part, last_in.at[k], last_send.at[k], last_recv.at[k], {"dom": peers[k]})
-        for k in range(1, slabs)
-    ]
+    last_copies = []
+
+    def send_scalars(curve):
+        alpha = norm / curve
+        later = r0[...] - alpha * w0[...]
+        three = jnp.where(
+            lane == 0,
+            dot(later, later),
+            jnp.where(
+                lane == 1,
+                dot(later, w0[...] - alpha * image[...]),
+                jnp.where(lane == 2, dot(later, w0[...]), 0.0),
+            ),
+        )
+        three = jnp.concatenate([three, jnp.zeros((128 - bands, 128), jnp.float32)], axis=0)
+        last_part[...] = lax.dot_general(
+            eye[0:8], three, NT, precision=HIGH, preferred_element_type=jnp.float32
+        )
+        last_copies.extend(
+            send(last_part, last_in.at[k], last_send.at[k], last_recv.at[k], {"dom": peers[k]})
+            for k in range(1, slabs)
+        )
+
+    curve, coefficients = apply(2, w0, dot(r0[...], w0[...]), send_scalars)
+    alpha = norm / curve
+    on_occupied = dot(totals[1] - alpha * totals[2], coefficients)
     value = last_part[...]
     for k in range(1, slabs):
         last_copies[k - 1].wait_recv()
@@ -644,7 +676,8 @@
     three = lax.dot_general(
         eye[0:bands], value, NT, precision=HIGH, preferred_element_type=jnp.float32
     )
-    new, bend, cross = three[:, 0:1], three[:, 1:2], three[:, 2:3]
+    new, cross = three[:, 0:1], three[:, 2:3]
+    bend = three[:, 1:2] - alpha * on_occupied
     ratio = new / norm
     step = new / (bend + ratio * (2.0 * cross + ratio * curve))
     weights[...] = jnp.where(
@@ -724,12 +757,10 @@
             pltpu.VMEM((3, slabs, 8, rows), f32),
             pltpu.VMEM((3, 8, rows), f32),
             pltpu.VMEM((3, bands, rows), f32),
-            pltpu.VMEM((8, every), f32),
-            pltpu.VMEM((slabs, 8, every), f32),
             pltpu.VMEM((8, 128), f32),
             pltpu.VMEM((slabs, 8, 128), f32),
-            dma((5,)),
-            dma((5,)),
+            dma((2 * PIECES + 1,)),
+            dma((2 * PIECES + 1,)),
             dma((3, CHUNKS)),
             dma((3, CHUNKS)),
             dma((3, CHUNKS)),
@@ -738,8 +769,6 @@
             dma((3, slabs)),
             dma((3, slabs)),
             dma((3, slabs)),
-            dma((slabs,)),
-            dma((slabs,)),
             dma((slabs,)),
             dma((slabs,)),
             dma((10,)),

time: 72.5 us -> 71.3 us (0.983)
  Pallas kernels: 71 us -> 69.9 us
    pallas_call x1, Pallas kernels: 70 us -> 68.8 us  [fused(): pl.pallas_call(functools.partial(fused_kernel, atoms, slabs), out_shape=(...]
where the time goes in v2:
time: 71.3 us; the launch traced here: 71.2 us
  Pallas kernels  69.9 us (98%)
  between operations  1.29 us (2%)
    pallas_call x1, Pallas kernels, fused(): pl.pallas_call(functools.partial(fused_kernel, atoms, slabs), out_shape=(...  68.8 us

profile of v2, /device:TPU:0, one launch (start us, length us, event | category | flops | bytes accessed | tf_op | source)
XLA Modules:
  0.0 71.2 jit_solution(10830452376679195779)
XLA Ops:
  1.3 68.8 %shard_map.122 = (f32[64,1536]{1,0:T(8,128)S(1)}, f32[64,1536]{1,0:T(8,128)S(1)}, f32[64,1536]{1,0:T(8,128)S(1)}, f32[64,1536]{1,0:T(8,128)S(1)}, f32[64,128]{1,0:T(8,128)S(1)}) custom-call(f32[64,1536]{1,0:T(8,128)} %occ_in.1, f32[64,1536]{1,0:T(8,128)} %bitcast.6, f32[12,128]{1,0:T(8,128)} %bitcast.7, f32[1,1536]{1,0:T(1,128)} %pert_in.1, ...), custom_call_target="tpu_custom_call" | custom-call | tf_op jit(solution)/shard_map/pallas_call | solution.py:731
  70.1 1.1 %shard_map.123 = (f32[1,64,1536]{2,1,0:T(8,128)}, f32[1,64,1536]{2,1,0:T(8,128)}) custom-call(f32[64,1536]{1,0:T(8,128)S(1)} %get-tuple-element.7.start, f32[64,1536]{1,0:T(8,128)S(1)} %get-tuple-element.8.r0, f32[64,1536]{1,0:T(8,128)S(1)} %get-tuple-element.9.w0, f32[64,1536]{1,0:T(8,128)S(1)} %get-tuple-element.10.z0, f32[64,128]{1,0:T(8,128)S(1)} %get-tuple-element.11.weights), custom_call_target="tpu_custom_call" | custom-call | tf_op jit(solution)/shard_map/pallas_call | solution.py:798

commit v3 on v2

--- a/solution.py
+++ b/solution.py
@@ -12,7 +12,7 @@
 PLANE = NY * NX
 HALO = 6
 CHUNKS = 8
-SUM_AT = 1
+SUM_AT = 2
 FINISH = 4
 PIECES = 4
 EAGER = 0
@@ -245,7 +245,9 @@
     def one(u, v):
         return lax.dot_general(u, v, dims, preferred_element_type=jnp.float32)
 
-    return one(a[0], b[0]) + (one(a[0], b[1]) + one(a[1], b[0]))
+    rows = a[0].shape[0]
+    both = one(jnp.concatenate(a, axis=0), b[0])
+    return both[:rows] + (one(a[0], b[1]) + both[rows:])
 
 
 def fused_kernel(
@@ -408,7 +410,7 @@
         f_high[...] = high
         f_low[...] = low
 
-    def plane_image(field, planes):
+    def plane_image(field, image, planes):
         for z in planes:
             cut = slice(z * PLANE, (z + 1) * PLANE)
             local_pot = jnp.concatenate(
@@ -418,7 +420,7 @@
                 (f_high[:, cut], f_low[:, cut]), (plane_high[...], plane_low[...]), NN
             ) + (local_pot - energy[:, 0:1]) * field[:, cut]
 
-    def across_planes(turn, field, c):
+    def across_planes(turn, field, image, c):
         def group(i, carry):
             rows = pl.ds(pl.multiple_of(i * 8, 8), 8)
             grid = [
@@ -483,14 +485,17 @@
     pair = slice(every, every + 128)
 
     def pair_part(q, block):
-        rows = slice(q * bands, (q + 1) * bands)
-        mine = product(
+        rows = slice(q * bands, (q + 2) * bands)
+        both = product(
             (w_high[rows, :], w_low[rows, :]), (w_high[pair, :], w_low[pair, :]), NT
         )
-        if q:
-            mine = pltpu.roll(mine, 2 * q, 1)
-        at = atoms + 2 * q
-        return jnp.where((lane == at) | (lane == at + 1), mine, block)
+        for i in range(2):
+            mine = both[i * bands : (i + 1) * bands]
+            if q + i:
+                mine = pltpu.roll(mine, 2 * (q + i), 1)
+            at = atoms + 2 * (q + i)
+            block = jnp.where((lane == at) | (lane == at + 1), mine, block)
+        return block
 
     one_cell = lax.broadcasted_iota(jnp.int32, (PLANE, PLANE), 0)
     other_cell = lax.broadcasted_iota(jnp.int32, (PLANE, PLANE), 1)
@@ -521,7 +526,7 @@
     hold(0, occ[...])
     hold(every, fields[...])
     hold_field(start[...])
-    plane_image(start, range(HALO))
+    plane_image(start, image, range(HALO))
     hand_on(0, moving, 0)
     hand_on(0, moving, 1)
     ends = slice(every, every + 128)
@@ -533,7 +538,7 @@
     hold(bands, whole[0])
     hand_on(0, moving, 3)
     part[0, :, 0 : 2 * bands] = correlate(slice(0, 2 * bands))
-    on_fields = pair_part(0, pair_part(1, on_start))
+    on_fields = pair_part(0, on_start)
     passed = []
     for c in range(PIECES):
         crossing[c].wait_recv()
@@ -554,12 +559,12 @@
     passed[PIECES - 1].wait_recv()
     hold(4 * bands - half, whole[2, bands - half :])
     part[0, :, 2 * bands : every] = correlate(slice(2 * bands, every))
-    part[0, :, every:] = pair_part(2, pair_part(3, on_fields))
+    part[0, :, every:] = pair_part(2, on_fields)
     copies = start_sum(0)
     shared = share_sum(0, copies)
     for c in range(CHUNKS):
         moving[CHUNKS + c].wait_recv()
-        across_planes(0, start, c)
+        across_planes(0, start, image, c)
     finish_sum(shared)
     last = totals[0, :, every:]
     own_radial, own_slope = last[:, atoms : atoms + 1], last[:, atoms + 1 : atoms + 2]
@@ -571,14 +576,15 @@
     )
     first = totals[0, :, 0:every] + STRENGTH * product(parts_of(swapped), parts_of(of_all), NT)
     ends_part = jnp.where(lane < atoms, last, swapped)
-    r0[...] = (
-        back(jnp.concatenate([first * (1.0 / total), -STRENGTH * ends_part], axis=1))
-        - image[...]
-        - pert[...] * occ[...]
-    )
-
-    def apply(turn, field, scalar, between=None):
-        face = [send_face(turn, field, c) for c in range(2)]
+    projected = back(jnp.concatenate([first * (1.0 / total), -STRENGTH * ends_part], axis=1))
+    early = []
+    for rows in (slice(0, 2 * chunk), slice(2 * chunk, bands)):
+        r0[rows] = projected[rows] - image[rows] - pert[...] * occ[rows]
+        if not early:
+            early = [send_face(1, r0, c) for c in range(2)]
+
+    def apply(turn, field, image, early, scalar, between=None):
+        face = list(early)
         hold_field(field[...])
         part[turn, :, 0:every] = correlate(slice(0, every))
         part[turn, :, every:] = jnp.where(lane == atoms, scalar, correlate(ends))
@@ -595,7 +601,7 @@
             for copy in face[2:DEPTH]:
                 copy.start()
 
-        plane_image(field, range(HALO))
+        plane_image(field, image, range(HALO))
         handed = []
         for c in range(CHUNKS):
             face[c].wait_recv()
@@ -610,12 +616,12 @@
                 shared = share_sum(turn, copies)
             if c >= 4:
                 handed[c - 4].wait_recv()
-                across_planes(turn, field, c - 4)
+                across_planes(turn, field, image, c - 4)
         finish_sum(shared)
         if between is not None:
             for c in range(CHUNKS - 4, CHUNKS):
                 handed[c].wait_recv()
-                across_planes(turn, field, c)
+                across_planes(turn, field, image, c)
             between(totals[turn, :, every + atoms : every + atoms + 1])
         last = totals[turn, :, every:]
         coefficients = jnp.concatenate(
@@ -627,16 +633,17 @@
         )
         image[...] += back(coefficients)
         if between is None:
+            ahead.extend(send_face(turn + 1, image, c) for c in range(2))
             for c in range(CHUNKS - 4, CHUNKS):
                 handed[c].wait_recv()
-                across_planes(turn, field, c)
+                across_planes(turn, field, image, c)
         return last[:, atoms : atoms + 1], coefficients
 
     def dot(u, v):
         return jnp.sum(u * v, axis=1, keepdims=True)
 
-    norm, _ = apply(1, r0, dot(r0[...], r0[...]))
-    w0[...] = image[...]
+    ahead = []
+    norm, _ = apply(1, r0, w0, early, dot(r0[...], r0[...]))
     eye = jnp.where(
         lax.broadcasted_iota(jnp.int32, (128, 128), 0)
         == lax.broadcasted_iota(jnp.int32, (128, 128), 1),
@@ -666,7 +673,7 @@
             for k in range(1, slabs)
         )
 
-    curve, coefficients = apply(2, w0, dot(r0[...], w0[...]), send_scalars)
+    curve, coefficients = apply(2, w0, image, ahead, dot(r0[...], w0[...]), send_scalars)
     alpha = norm / curve
     on_occupied = dot(totals[1] - alpha * totals[2], coefficients)
     value = last_part[...]

time: 71.3 us -> 69.2 us (0.971)
  Pallas kernels: 69.9 us -> 67.7 us
    pallas_call x1, Pallas kernels: 68.8 us -> 66.7 us  [fused(): pl.pallas_call(functools.partial(fused_kernel, atoms, slabs), out_shape=(...]
where the time goes in v3:
time: 69.2 us; the launch traced here: 69 us
  Pallas kernels  67.7 us (98%)
  between operations  1.29 us (2%)
    pallas_call x1, Pallas kernels, fused(): pl.pallas_call(functools.partial(fused_kernel, atoms, slabs), out_shape=(...  66.7 us

profile of v3, /device:TPU:0, one launch (start us, length us, event | category | flops | bytes accessed | tf_op | source)
XLA Modules:
  0.0 69.0 jit_solution(15719160510065267603)
XLA Ops:
  1.3 66.7 %shard_map.122 = (f32[64,1536]{1,0:T(8,128)S(1)}, f32[64,1536]{1,0:T(8,128)S(1)}, f32[64,1536]{1,0:T(8,128)S(1)}, f32[64,1536]{1,0:T(8,128)S(1)}, f32[64,128]{1,0:T(8,128)S(1)}) custom-call(f32[64,1536]{1,0:T(8,128)} %occ_in.1, f32[64,1536]{1,0:T(8,128)} %bitcast.6, f32[12,128]{1,0:T(8,128)} %bitcast.7, f32[1,1536]{1,0:T(1,128)} %pert_in.1, ...), custom_call_target="tpu_custom_call" | custom-call | tf_op jit(solution)/shard_map/pallas_call | solution.py:738
  68.0 1.1 %shard_map.123 = (f32[1,64,1536]{2,1,0:T(8,128)}, f32[1,64,1536]{2,1,0:T(8,128)}) custom-call(f32[64,1536]{1,0:T(8,128)S(1)} %get-tuple-element.7.start, f32[64,1536]{1,0:T(8,128)S(1)} %get-tuple-element.8.r0, f32[64,1536]{1,0:T(8,128)S(1)} %get-tuple-element.9.w0, f32[64,1536]{1,0:T(8,128)S(1)} %get-tuple-element.10.z0, f32[64,128]{1,0:T(8,128)S(1)} %get-tuple-element.11.weights), custom_call_target="tpu_custom_call" | custom-call | tf_op jit(solution)/shard_map/pallas_call | solution.py:805

commit v4 on v3

--- a/solution.py
+++ b/solution.py
@@ -16,7 +16,7 @@
 FINISH = 4
 PIECES = 4
 EAGER = 0
-DEPTH = 3
+DEPTH = 5
 RAD = 5
 
 COEF = (
@@ -578,27 +578,33 @@
     ends_part = jnp.where(lane < atoms, last, swapped)
     projected = back(jnp.concatenate([first * (1.0 / total), -STRENGTH * ends_part], axis=1))
     early = []
-    for rows in (slice(0, 2 * chunk), slice(2 * chunk, bands)):
+    for rows in (slice(0, 3 * chunk), slice(3 * chunk, bands)):
         r0[rows] = projected[rows] - image[rows] - pert[...] * occ[rows]
         if not early:
-            early = [send_face(1, r0, c) for c in range(2)]
-
-    def apply(turn, field, image, early, scalar, between=None):
+            early = [send_face(1, r0, c) for c in range(3)]
+
+    def dot(u, v):
+        return jnp.sum(u * v, axis=1, keepdims=True)
+
+    def apply(turn, field, image, early, between=None):
         face = list(early)
         hold_field(field[...])
-        part[turn, :, 0:every] = correlate(slice(0, every))
-        part[turn, :, every:] = jnp.where(lane == atoms, scalar, correlate(ends))
+        on_all = correlate(slice(0, every + 128))
+        part[turn, :, 0:every] = on_all[:, 0:every]
+        part[turn, :, every:] = jnp.where(
+            lane == atoms, dot(r0[...], field[...]), on_all[:, every:]
+        )
         copies = start_sum(turn)
-        face += [send_face(turn, field, c, False) for c in range(2, CHUNKS)]
+        face += [send_face(turn, field, c, False) for c in range(3, CHUNKS)]
 
         @pl.when(band % 2 == EAGER)
         def _():
-            for copy in face[2:]:
+            for copy in face[3:]:
                 copy.start()
 
         @pl.when(band % 2 != EAGER)
         def _():
-            for copy in face[2:DEPTH]:
+            for copy in face[3:DEPTH]:
                 copy.start()
 
         plane_image(field, image, range(HALO))
@@ -633,17 +639,14 @@
         )
         image[...] += back(coefficients)
         if between is None:
-            ahead.extend(send_face(turn + 1, image, c) for c in range(2))
+            ahead.extend(send_face(turn + 1, image, c) for c in range(3))
             for c in range(CHUNKS - 4, CHUNKS):
                 handed[c].wait_recv()
                 across_planes(turn, field, image, c)
         return last[:, atoms : atoms + 1], coefficients
 
-    def dot(u, v):
-        return jnp.sum(u * v, axis=1, keepdims=True)
-
     ahead = []
-    norm, _ = apply(1, r0, w0, early, dot(r0[...], r0[...]))
+    norm, _ = apply(1, r0, w0, early)
     eye = jnp.where(
         lax.broadcasted_iota(jnp.int32, (128, 128), 0)
         == lax.broadcasted_iota(jnp.int32, (128, 128), 1),
@@ -673,7 +676,7 @@
             for k in range(1, slabs)
         )
 
-    curve, coefficients = apply(2, w0, image, ahead, dot(r0[...], w0[...]), send_scalars)
+    curve, coefficients = apply(2, w0, image, ahead, send_scalars)
     alpha = norm / curve
     on_occupied = dot(totals[1] - alpha * totals[2], coefficients)
     value = last_part[...]

time: 69.2 us -> 68.6 us (level)
  no operation moved by 1% of the time
where the time goes in v4:
time: 68.6 us; the launch traced here: 68.4 us
  Pallas kernels  67.2 us (98%)
  between operations  1.29 us (2%)
    pallas_call x1, Pallas kernels, fused(): pl.pallas_call(functools.partial(fused_kernel, atoms, slabs), out_shape=(...  66.1 us

profile of v4, /device:TPU:0, one launch (start us, length us, event | category | flops | bytes accessed | tf_op | source)
XLA Modules:
  0.0 68.4 jit_solution(12752862194722563480)
XLA Ops:
  1.3 66.1 %shard_map.122 = (f32[64,1536]{1,0:T(8,128)S(1)}, f32[64,1536]{1,0:T(8,128)S(1)}, f32[64,1536]{1,0:T(8,128)S(1)}, f32[64,1536]{1,0:T(8,128)S(1)}, f32[64,128]{1,0:T(8,128)S(1)}) custom-call(f32[64,1536]{1,0:T(8,128)} %occ_in.1, f32[64,1536]{1,0:T(8,128)} %bitcast.6, f32[12,128]{1,0:T(8,128)} %bitcast.7, f32[1,1536]{1,0:T(1,128)} %pert_in.1, ...), custom_call_target="tpu_custom_call" | custom-call | tf_op jit(solution)/shard_map/pallas_call | solution.py:741
  67.4 1.1 %shard_map.123 = (f32[1,64,1536]{2,1,0:T(8,128)}, f32[1,64,1536]{2,1,0:T(8,128)}) custom-call(f32[64,1536]{1,0:T(8,128)S(1)} %get-tuple-element.7.start, f32[64,1536]{1,0:T(8,128)S(1)} %get-tuple-element.8.r0, f32[64,1536]{1,0:T(8,128)S(1)} %get-tuple-element.9.w0, f32[64,1536]{1,0:T(8,128)S(1)} %get-tuple-element.10.z0, f32[64,128]{1,0:T(8,128)S(1)} %get-tuple-element.11.weights), custom_call_target="tpu_custom_call" | custom-call | tf_op jit(solution)/shard_map/pallas_call | solution.py:808

commit v5 on v4

--- a/solution.py
+++ b/solution.py
@@ -623,9 +623,11 @@
             if c >= 4:
                 handed[c - 4].wait_recv()
                 across_planes(turn, field, image, c - 4)
+        handed[CHUNKS - 4].wait_recv()
+        across_planes(turn, field, image, CHUNKS - 4)
         finish_sum(shared)
         if between is not None:
-            for c in range(CHUNKS - 4, CHUNKS):
+            for c in range(CHUNKS - 3, CHUNKS):
                 handed[c].wait_recv()
                 across_planes(turn, field, image, c)
             between(totals[turn, :, every + atoms : every + atoms + 1])
@@ -640,7 +642,7 @@
         image[...] += back(coefficients)
         if between is None:
             ahead.extend(send_face(turn + 1, image, c) for c in range(3))
-            for c in range(CHUNKS - 4, CHUNKS):
+            for c in range(CHUNKS - 3, CHUNKS):
                 handed[c].wait_recv()
                 across_planes(turn, field, image, c)
         return last[:, atoms : atoms + 1], coefficients

time: 68.6 us -> 68.2 us (level)
  no operation moved by 1% of the time
where the time goes in v5:
time: 68.2 us; the launch traced here: 68.1 us
  Pallas kernels  66.8 us (98%)
  between operations  1.29 us (2%)
    pallas_call x1, Pallas kernels, fused(): pl.pallas_call(functools.partial(fused_kernel, atoms, slabs), out_shape=(...  65.7 us

profile of v5, /device:TPU:0, one launch (start us, length us, event | category | flops | bytes accessed | tf_op | source)
XLA Modules:
  0.0 68.1 jit_solution(8025165500443097200)
XLA Ops:
  1.3 65.7 %shard_map.122 = (f32[64,1536]{1,0:T(8,128)S(1)}, f32[64,1536]{1,0:T(8,128)S(1)}, f32[64,1536]{1,0:T(8,128)S(1)}, f32[64,1536]{1,0:T(8,128)S(1)}, f32[64,128]{1,0:T(8,128)S(1)}) custom-call(f32[64,1536]{1,0:T(8,128)} %occ_in.1, f32[64,1536]{1,0:T(8,128)} %bitcast.6, f32[12,128]{1,0:T(8,128)} %bitcast.7, f32[1,1536]{1,0:T(1,128)} %pert_in.1, ...), custom_call_target="tpu_custom_call" | custom-call | tf_op jit(solution)/shard_map/pallas_call | solution.py:743
  67.0 1.1 %shard_map.123 = (f32[1,64,1536]{2,1,0:T(8,128)}, f32[1,64,1536]{2,1,0:T(8,128)}) custom-call(f32[64,1536]{1,0:T(8,128)S(1)} %get-tuple-element.7.start, f32[64,1536]{1,0:T(8,128)S(1)} %get-tuple-element.8.r0, f32[64,1536]{1,0:T(8,128)S(1)} %get-tuple-element.9.w0, f32[64,1536]{1,0:T(8,128)S(1)} %get-tuple-element.10.z0, f32[64,128]{1,0:T(8,128)S(1)} %get-tuple-element.11.weights), custom_call_target="tpu_custom_call" | custom-call | tf_op jit(solution)/shard_map/pallas_call | solution.py:810

commit v6 on v5

--- a/solution.py
+++ b/solution.py
@@ -639,9 +639,12 @@
             ],
             axis=1,
         )
-        image[...] += back(coefficients)
+        projected = back(coefficients)
+        for rows in (slice(0, 3 * chunk), slice(3 * chunk, bands)):
+            image[rows] += projected[rows]
+            if between is None and not ahead:
+                ahead.extend(send_face(turn + 1, image, c) for c in range(3))
         if between is None:
-            ahead.extend(send_face(turn + 1, image, c) for c in range(3))
             for c in range(CHUNKS - 3, CHUNKS):
                 handed[c].wait_recv()
                 across_planes(turn, field, image, c)

time: 68.2 us -> 68.2 us (level)
  no operation moved by 1% of the time
where the time goes in v6:
time: 68.2 us; the launch traced here: 68 us
  Pallas kernels  66.8 us (98%)
  between operations  1.29 us (2%)
    pallas_call x1, Pallas kernels, fused(): pl.pallas_call(functools.partial(fused_kernel, atoms, slabs), out_shape=(...  65.7 us

profile of v6, /device:TPU:0, one launch (start us, length us, event | category | flops | bytes accessed | tf_op | source)
XLA Modules:
  0.0 68.0 jit_solution(9464701499560888437)
XLA Ops:
  1.3 65.7 %shard_map.122 = (f32[64,1536]{1,0:T(8,128)S(1)}, f32[64,1536]{1,0:T(8,128)S(1)}, f32[64,1536]{1,0:T(8,128)S(1)}, f32[64,1536]{1,0:T(8,128)S(1)}, f32[64,128]{1,0:T(8,128)S(1)}) custom-call(f32[64,1536]{1,0:T(8,128)} %occ_in.1, f32[64,1536]{1,0:T(8,128)} %bitcast.6, f32[12,128]{1,0:T(8,128)} %bitcast.7, f32[1,1536]{1,0:T(1,128)} %pert_in.1, ...), custom_call_target="tpu_custom_call" | custom-call | tf_op jit(solution)/shard_map/pallas_call | solution.py:746
  67.0 1.1 %shard_map.123 = (f32[1,64,1536]{2,1,0:T(8,128)}, f32[1,64,1536]{2,1,0:T(8,128)}) custom-call(f32[64,1536]{1,0:T(8,128)S(1)} %get-tuple-element.7.start, f32[64,1536]{1,0:T(8,128)S(1)} %get-tuple-element.8.r0, f32[64,1536]{1,0:T(8,128)S(1)} %get-tuple-element.9.w0, f32[64,1536]{1,0:T(8,128)S(1)} %get-tuple-element.10.z0, f32[64,128]{1,0:T(8,128)S(1)} %get-tuple-element.11.weights), custom_call_target="tpu_custom_call" | custom-call | tf_op jit(solution)/shard_map/pallas_call | solution.py:813
